TPU v7x, 256 devices: a whole 4x4x8 slice. The times are simulated.
256 devices in a mesh: dp: 32 (over y, x, core), tensor: 8 (over z).
Axes of the slice: x: 4, y: 4, z: 8, core: 2. Of those that a mesh axis runs over, the one named last changes fastest.
Arguments:
- inputs: bfloat16 [16384, 2560], P('dp'), may hold values from -6 to 6
- cotangent: bfloat16 [16384, 13312], P('dp', 'tensor'), may hold values from -48 to 48
- seed_values: int32 [13312, 32], P('tensor'), may hold values from -64 to 64
- counts: int32 [32], P('dp'), may hold values from 1 to 512, 8192 in all
Outputs:
- new_error: bfloat16 [32, 2560, 13312], P('dp', None, 'tensor')
- q_factor: float32 [13312, 32], P('tensor')
Inputs may be any that keep to these rules, and one draw needn't show every extreme that they name: `counts`: each replica has at least one live token; some replica fills all 512 slots.
All inputs are finite; a program needn't handle non-finite values. No bound on the sum of `counts` on one device may be relied on, other than what follows from the above.
Results may differ from a plain program's by a relative error of at most 0.001.
Values sent between devices are 32-bit elements; how exact they have to be, the bound alone decides.
A program may use at most 128 MiB of HBM per device.

v0:
```python
import jax
import jax.numpy as jnp
from jax import lax
from jax.sharding import PartitionSpec as P


def orthonormal(matrix):
    cols = matrix.shape[1]
    places = jnp.arange(cols)

    def orth_step(column_index, current):
        column = lax.dynamic_slice_in_dim(current, column_index, 1, 1)
        earlier = (places < column_index).astype(jnp.float32)[:, None]
        for repeat in range(2):
            coeffs = jnp.dot(current.T, column, precision=lax.Precision.HIGHEST) * earlier
            column = column - jnp.dot(current, coeffs, precision=lax.Precision.HIGHEST)
        column = column / jnp.sqrt(jnp.sum(column * column))
        return lax.dynamic_update_slice_in_dim(current, column, column_index, 1)

    return lax.fori_loop(0, cols, orth_step, matrix)


def shards(inputs, cotangent, seed_values, counts):
    replicas = lax.axis_size("dp")
    positions = lax.broadcasted_iota(jnp.int32, (inputs.shape[0], 1), 0)
    live_inputs = jnp.where(positions < counts[0], inputs, jnp.zeros_like(inputs))
    weight_grad = jnp.dot(live_inputs.T, cotangent, preferred_element_type=jnp.float32)
    start_factor = seed_values.astype(jnp.float32) / 64.0
    p_local = jnp.dot(weight_grad, start_factor, precision=lax.Precision.HIGHEST)
    p_summed = lax.psum(p_local, ("dp", "tensor"))
    ortho_basis = orthonormal(p_summed)
    q_local = jnp.dot(weight_grad.T, ortho_basis, precision=lax.Precision.HIGHEST)
    token_count = lax.psum(counts[0], "dp").astype(jnp.float32)
    grad_scale = replicas / token_count
    q_factor = lax.psum(q_local * grad_scale, "dp") / replicas
    approx = jnp.dot(ortho_basis, q_factor.T, precision=lax.Precision.HIGHEST)
    new_error = (weight_grad * grad_scale - approx).astype(jnp.bfloat16)
    return (new_error[None], q_factor)


def solution(mesh):
    return jax.shard_map(
        shards,
        mesh=mesh,
        in_specs=(P("dp", None), P("dp", "tensor"), P("tensor", None), P("dp")),
        out_specs=(P("dp", None, "tensor"), P("tensor", None)),
        check_vma=False,
    )
```

profile of v0, /device:TPU:1, one launch (start us, length us, event | category | flops | bytes accessed | tf_op | source)
XLA Modules:
  0.0 697.5 jit_solution(8392071743485835729)
XLA Ops:
  8.6 6.8 fusion.11
  15.5 5.8 copy-done.1
  21.3 16.7 %fusion.15 = f32[2560,32]{0,1:T(8,128)} fusion(f32[2560,1664]{1,0:T(8,128)S(1)} %fusion.11, s32[1664,32]{0,1:T(8,128)S(1)} %copy-done.4), kind=kOutput, calls=%fused_computation.22 | convolution fusion | flops 1635885056 | bytes 17580032 | tf_op jit(solution)/shard_map/dot_general | solution.py:29
  38.1 15.1 %psum.21 = s32[]{:T(128)} all-reduce(s32[]{:T(128)} %bitcast), channel_id=1, replica_groups=mesh['dp'=32,'tensor'=8] {'dp'}, use_global_device_ids=true, to_apply=%region_0.1 | all-reduce | flops 1 | bytes 8 | tf_op jit(solution)/shard_map/psum | solution.py:33
  53.8 234.2 %all-reduce.3.cloned.1.call-done = f32[2560,32]{0,1:T(8,128)} async-done(((f32[2560,32]{0,1:T(8,128)}), f32[2560,32]{0,1:T(8,128)}) %all-reduce.3.cloned.1.call-update) | async-done | bytes 327696 | tf_op jit(solution)/shard_map/psum | solution.py:30
  288.0 261.4 %while.14 = (s32[]{:T(128)}, f32[2560,32]{0,1:T(8,128)}, s32[]{:T(128)}, s32[]{:T(128)}) while((s32[]{:T(128)}, f32[2560,32]{0,1:T(8,128)}, s32[]{:T(128)}, s32[]{:T(128)}) %tuple.39), condition=%wide.region_4.5_spmd.clone, body=%wide.region_2.4_spmd.clone.sunk | while | flops 3945089 | bytes 1414745 | solution.py:20
  292.0 1.9 multiply_reduce_fusion.2
  300.2 1.9 multiply_reduce_fusion.2
  316.5 1.9 multiply_reduce_fusion.2
  324.7 1.9 multiply_reduce_fusion.2
  332.9 1.9 multiply_reduce_fusion.2
  341.0 1.9 multiply_reduce_fusion.2
  365.6 1.9 multiply_reduce_fusion.2
  381.9 1.9 multiply_reduce_fusion.2
  398.2 1.9 multiply_reduce_fusion.2
  406.4 1.9 multiply_reduce_fusion.2
  422.7 1.9 multiply_reduce_fusion.2
  439.0 1.9 multiply_reduce_fusion.2
  512.5 1.9 multiply_reduce_fusion.2
  528.9 1.9 multiply_reduce_fusion.2
  545.2 1.9 multiply_reduce_fusion.2
  549.4 13.6 %convolution_multiply_fusion = f32[1664,32]{0,1:T(8,128)} fusion(f32[2560,1664]{1,0:T(8,128)} %copy-done.1, f32[2560,32]{0,1:T(8,128)} %get-tuple-element.66, f32[]{:T(128)S(6)} %div.29), kind=kOutput, calls=%fused_computation.20 | convolution fusion | flops 1635831808 | bytes 17580036 | tf_op jit(solution)/shard_map/dot_general | solution.py:32
  563.0 108.5 %all-reduce.5.cloned.1.call-done = f32[1664,32]{0,1:T(8,128)} async-done(((f32[1664,32]{0,1:T(8,128)}), f32[1664,32]{0,1:T(8,128)}) %all-reduce.5.cloned.1.call-update) | async-done | bytes 213008 | tf_op jit(solution)/shard_map/psum | solution.py:35
  672.5 18.2 %fusion.10 = bf16[1,2560,1664]{2,1,0:T(8,128)(2,1)} fusion(f32[2560,32]{0,1:T(8,128)S(1)} %copy-done.2, f32[1664,32]{0,1:T(8,128)S(1)} %broadcast_multiply_fusion, f32[2560,1664]{1,0:T(8,128)} %copy-done.1, f32[]{:T(128)S(6)} %div.29), kind=kOutput, calls=%fused_computation.16 | convolution fusion | flops 1648558080 | bytes 26099716 | tf_op jit(solution)/shard_map/dot_general | solution.py:36
  (192 shorter events, 211.9 us)
Async XLA Ops:
  7.2 1.5 copy-start
  7.2 14.1 %copy-start.4 = (s32[1664,32]{0,1:T(8,128)S(1)}, s32[1664,32]{0,1:T(8,128)}, u32[]{:S(2)}) copy-start(s32[1664,32]{0,1:T(8,128)} %param.8) | copy-start | bytes 638980
  7.2 280.8 %all-reduce.3.cloned.1.call-start = ((), (), s32[]{:S(2)}) async-start(), calls=%async_computation | async-start | bytes 655360 | tf_op jit(solution)/shard_map/psum | solution.py:30
  15.5 5.8 copy-start.1
  38.0 633.5 %all-reduce.5.cloned.1.call-start = ((), (), s32[]{:S(2)}) async-start(), calls=%async_computation.1 | async-start | bytes 425984 | tf_op jit(solution)/shard_map/psum | solution.py:35
  549.4 123.1 %copy-start.2 = (f32[2560,32]{0,1:T(8,128)S(1)}, f32[2560,32]{0,1:T(8,128)}, u32[]{:S(2)}) copy-start(f32[2560,32]{0,1:T(8,128)} %get-tuple-element.66) | copy-start | bytes 983044
  672.5 18.2 %copy-start.3 = (f32[1664,32]{0,1:T(8,128)}, f32[1664,32]{0,1:T(8,128)S(1)}, u32[]{:S(2)}) copy-start(f32[1664,32]{0,1:T(8,128)S(1)} %broadcast_multiply_fusion) | copy-start | bytes 638980
Sparse Core Ops, SparseCore 0:
  38.1 249.7 all-reduce.2
  563.1 108.3 all-reduce.4
where the time goes:
time: 703 us; the launch traced here: 698 us
  waiting for transfers between devices  343 us (49%)
  matrix products  244 us (35%)
  local copies, waits for them, and re-layouts  56.2 us (8%)
  loops' own time  22.7 us (3%)
  between operations  15.5 us (2%)
  blocking collectives  15.1 us (2%)
    psum x1, waiting for transfers between devices, shards(): p_summed = lax.psum(p_local, ('dp', 'tensor'))  234 us
    psum x1, waiting for transfers between devices, shards(): q_factor = lax.psum(q_local * grad_scale, 'dp') / replicas  108 us
    dot_general x64, matrix products, orth_step(): column = column - jnp.dot(current, coeffs, precision=lax.Precision.HIGHEST)  102 us
    dot_general x64, matrix products, orth_step(): jnp.dot(current.T, column, precision=lax.Precision.HIGHEST) * earlier  86.1 us
    dynamic_update_slice x32, local copies, waits for them, and re-layouts, orth_step(): return lax.dynamic_update_slice_in_dim(current, column, column_index, 1)  49.8 us
    another operation x1, loops' own time, orthonormal(): return lax.fori_loop(0, cols, orth_step, matrix)  22.7 us
    dot_general x1, matrix products, shards(): approx = jnp.dot(ortho_basis, q_factor.T, precision=lax.Precision.HIGHEST)  18.2 us
    dot_general x1, matrix products, shards(): jnp.dot(weight_grad, start_factor, precision=lax.Precision.HIGHEST)  16.7 us
  transfers between devices with their start and end apart: 2, of which 2 were waited for; matrix products, arithmetic and copies ran while one was open for 0% of the time, Pallas kernels for 0%

commit v1 on v0

v1 whole, which is shorter than its diff:
```python
import functools

import jax
import jax.numpy as jnp
from jax import lax
from jax.experimental import pallas as pl
from jax.experimental.pallas import tpu as pltpu
from jax.sharding import PartitionSpec as P

F32, BF16 = jnp.float32, jnp.bfloat16
LANES = 128
NT = (((1,), (1,)), ((), ()))
TN = (((0,), (0,)), ((), ()))


def round_up(value, unit):
    return -(-value // unit) * unit


def split3(value):
    high = value.astype(BF16)
    rest = value - high.astype(F32)
    mid = rest.astype(BF16)
    low = (rest - mid.astype(F32)).astype(BF16)
    return high, mid, low


def fold3(stacked):
    rows = stacked.shape[0] // 3
    return stacked[:rows] + stacked[rows : 2 * rows] + stacked[2 * rows :]


def exact_dot(left, right, dims=(((1,), (0,)), ((), ()))):
    return lax.dot_general(left, right, dims, precision=lax.Precision.HIGHEST, preferred_element_type=F32)


def inverse_cholesky(gram):
    size = gram.shape[0]
    row = lax.broadcasted_iota(jnp.int32, (size, size), 0)
    col = lax.broadcasted_iota(jnp.int32, (size, size), 1)
    left, right = gram, (row == col).astype(F32)
    below = lax.broadcasted_iota(jnp.int32, (size, 1), 0)
    for k in range(size - 1):
        pivot = left[k : k + 1, k : k + 1]
        factor = jnp.where(below > k, left[:, k : k + 1] / pivot, 0.0)
        left, right = left - factor * left[k : k + 1, :], right - factor * right[k : k + 1, :]
    diagonal = jnp.sum(jnp.where(row == col, left, 0.0), axis=1, keepdims=True)
    guess = lax.rsqrt(diagonal)
    guess = guess * (1.5 - 0.5 * diagonal * guess * guess)
    return right * guess


def spread(ref, value, pitch):
    rows, width = value.shape
    for j in range(width // LANES):
        ref[pl.ds(j, rows, stride=pitch), :] = value[:, j * LANES : (j + 1) * LANES]


def collect(ref, rows, width, pitch):
    return jnp.concatenate([ref[pl.ds(j, rows, stride=pitch), :] for j in range(width // LANES)], axis=1)


def add_blocks(ref, blocks, pitch):
    total = ref[0:pitch, :]
    for i in range(1, blocks):
        total = total + ref[i * pitch : (i + 1) * pitch, :]
    return total


def exchange_kernel(
    n, nz, pitch_p, pitch_w,
    count_ref, x_hbm, c_hbm, s_hbm,
    basis_ref, qcat_ref, qt_ref, scale_ref,
    x, c, s, snd1, rcv1, zsnd, zrcv, pfull, snd2, rcv2, wfull,
    load_sem, send_sem, recv_sem,
):
    me, mz = lax.axis_index("dp"), lax.axis_index("tensor")
    tokens, d = x.shape
    f = c.shape[1]

    loads = [pltpu.make_async_copy(src, dst, load_sem.at[i]) for i, (src, dst) in enumerate(((c_hbm, c), (s_hbm, s), (x_hbm, x)))]
    for load in loads:
        load.start()

    barrier = pltpu.get_barrier_semaphore()

    @pl.loop(1, n)
    def _(k):
        pl.semaphore_signal(barrier, inc=1, device_id={"dp": lax.rem(me + k, n)}, device_id_type=pl.DeviceIdType.MESH)

    @pl.loop(1, nz)
    def _(k):
        pl.semaphore_signal(barrier, inc=1, device_id={"tensor": lax.rem(mz + k, nz)}, device_id_type=pl.DeviceIdType.MESH)

    def block(ref, index, pitch):
        return ref.at[pl.ds(pl.multiple_of(index * pitch, 8), pitch), :]

    def send(phase, axis, size, place, source, target):
        @pl.loop(1, size)
        def _(k):
            peer = lax.rem(place + k, size)
            pltpu.make_async_remote_copy(
                src_ref=source(peer), dst_ref=target, send_sem=send_sem.at[phase], recv_sem=recv_sem.at[phase],
                device_id={axis: peer}, device_id_type=pl.DeviceIdType.MESH,
            ).start()

    def wait(sem, ref, rows):
        part = ref.at[pl.ds(0, rows), :]
        pltpu.make_async_copy(part, part, sem).wait()

    live = lax.broadcasted_iota(jnp.int32, (n, tokens), 1) < count_ref[0]

    loads[0].wait()
    loads[1].wait()
    narrow = lax.dot_general(s[...].astype(F32).astype(BF16), c[...], NT, preferred_element_type=F32)
    narrow = jnp.concatenate(split3(jnp.where(live, narrow, 0.0)), axis=0)
    loads[2].wait()
    spread(snd1, fold3(jnp.dot(narrow, x[...], preferred_element_type=F32)), pitch_p)
    counted = jnp.full((n, LANES), count_ref[0], jnp.int32).astype(F32)
    snd1[pl.ds(d // LANES, n, stride=pitch_p), :] = counted
    for j in range(d // LANES + 1, pitch_p):
        snd1[pl.ds(j, n, stride=pitch_p), :] = jnp.zeros((n, LANES), F32)
    rcv1[pl.ds(pl.multiple_of(me * pitch_p, 8), pitch_p), :] = snd1[pl.ds(pl.multiple_of(me * pitch_p, 8), pitch_p), :]

    pl.semaphore_wait(barrier, n - 1 + nz - 1)
    send(0, "dp", n, me, lambda peer: block(snd1, peer, pitch_p), block(rcv1, me, pitch_p))
    wait(recv_sem.at[0], rcv1, (n - 1) * pitch_p)

    total = add_blocks(rcv1, n, pitch_p)
    token_count = total[d // LANES : d // LANES + 1, :]
    mine = total / (64.0 * token_count)
    zsnd[...] = mine
    zrcv[pl.ds(pl.multiple_of(mz * pitch_p, 8), pitch_p), :] = mine
    send(1, "tensor", nz, mz, lambda peer: zsnd, block(zrcv, mz, pitch_p))
    wait(recv_sem.at[1], zrcv, (nz - 1) * pitch_p)

    pfull[pl.ds(pl.multiple_of(me * pitch_p, 8), pitch_p), :] = add_blocks(zrcv, nz, pitch_p)
    send(2, "dp", n, me, lambda peer: block(pfull, me, pitch_p), block(pfull, me, pitch_p))
    wait(recv_sem.at[2], pfull, (n - 1) * pitch_p)

    left = collect(pfull, n, d, pitch_p)
    projected = fold3(lax.dot_general(jnp.concatenate(split3(left), axis=0), x[...], NT, preferred_element_type=F32))
    projected = jnp.concatenate(split3(jnp.where(live, projected, 0.0)), axis=0)
    spread(snd2, fold3(jnp.dot(projected, c[...], preferred_element_type=F32)), pitch_w)
    for j in range(f // LANES, pitch_w):
        snd2[pl.ds(j, n, stride=pitch_w), :] = jnp.zeros((n, LANES), F32)
    rcv2[pl.ds(pl.multiple_of(me * pitch_w, 8), pitch_w), :] = snd2[pl.ds(pl.multiple_of(me * pitch_w, 8), pitch_w), :]
    send(3, "dp", n, me, lambda peer: block(snd2, peer, pitch_w), block(rcv2, me, pitch_w))

    first = inverse_cholesky(exact_dot(left, left, NT))
    nearly = exact_dot(first, left)

    wait(recv_sem.at[3], rcv2, (n - 1) * pitch_w)
    wfull[pl.ds(pl.multiple_of(me * pitch_w, 8), pitch_w), :] = add_blocks(rcv2, n, pitch_w) / token_count
    send(4, "dp", n, me, lambda peer: block(wfull, me, pitch_w), block(wfull, me, pitch_w))

    second = inverse_cholesky(exact_dot(nearly, nearly, NT))
    basis = exact_dot(second, nearly)
    whole = exact_dot(second, first)
    h, m, l = split3(basis)
    basis_ref[...] = jnp.concatenate((h, h, m, h, l, m), axis=0)
    scale_ref[...] = jnp.broadcast_to(float(n) / token_count, scale_ref.shape)

    wait(recv_sem.at[4], wfull, (n - 1) * pitch_w)
    q = exact_dot(whole, collect(wfull, n, f, pitch_w))
    qt_ref[...] = q
    h, m, l = split3(q)
    qcat_ref[...] = jnp.concatenate((h, m, h, l, h, m), axis=0)

    wait(send_sem.at[0], snd1, (n - 1) * pitch_p)
    wait(send_sem.at[1], zrcv, (nz - 1) * pitch_p)
    wait(send_sem.at[2], pfull, (n - 1) * pitch_p)
    wait(send_sem.at[3], snd2, (n - 1) * pitch_w)
    wait(send_sem.at[4], wfull, (n - 1) * pitch_w)


def error_kernel(count_ref, x_ref, c_ref, basis_ref, qcat_ref, scale_ref, qt_in, out_ref, qt_out, live_c):
    @pl.when(pl.program_id(0) == 0)
    def _():
        position = lax.broadcasted_iota(jnp.int32, live_c.shape, 0)
        live_c[...] = jnp.where(position < count_ref[0], c_ref[...], jnp.zeros_like(c_ref))
        qt_out[...] = qt_in[...]

    grad = lax.dot_general(x_ref[...], live_c[...], TN, preferred_element_type=F32)
    approx = lax.dot_general(basis_ref[...], qcat_ref[...], TN, preferred_element_type=F32)
    out_ref[...] = (grad * scale_ref[0:1, 0:1] - approx).astype(BF16)


def shards(inputs, cotangent, seed_values, counts):
    n, nz = lax.axis_size("dp"), lax.axis_size("tensor")
    tokens, d = inputs.shape
    f = cotangent.shape[1]
    rank = seed_values.shape[1]
    pitch_p, pitch_w = round_up(d // LANES + 1, 8), round_up(f // LANES, 8)
    smem, anywhere = pl.BlockSpec(memory_space=pltpu.SMEM), pl.BlockSpec(memory_space=pl.ANY)
    vmem = pl.BlockSpec(memory_space=pltpu.VMEM)
    basis, qcat, qt, scale = pl.pallas_call(
        functools.partial(exchange_kernel, n, nz, pitch_p, pitch_w),
        out_shape=(
            jax.ShapeDtypeStruct((6 * rank, d), BF16),
            jax.ShapeDtypeStruct((6 * rank, f), BF16),
            jax.ShapeDtypeStruct((rank, f), F32),
            jax.ShapeDtypeStruct((8, LANES), F32),
        ),
        in_specs=[smem, anywhere, anywhere, anywhere],
        out_specs=(vmem,) * 4,
        scratch_shapes=[
            pltpu.VMEM((tokens, d), BF16),
            pltpu.VMEM((tokens, f), BF16),
            pltpu.VMEM((rank, f), jnp.int32),
            pltpu.VMEM((n * pitch_p, LANES), F32),
            pltpu.VMEM((n * pitch_p, LANES), F32),
            pltpu.VMEM((pitch_p, LANES), F32),
            pltpu.VMEM((nz * pitch_p, LANES), F32),
            pltpu.VMEM((n * pitch_p, LANES), F32),
            pltpu.VMEM((n * pitch_w, LANES), F32),
            pltpu.VMEM((n * pitch_w, LANES), F32),
            pltpu.VMEM((n * pitch_w, LANES), F32),
            pltpu.SemaphoreType.DMA((3,)),
            pltpu.SemaphoreType.DMA((5,)),
            pltpu.SemaphoreType.DMA((5,)),
        ],
        compiler_params=pltpu.CompilerParams(collective_id=0, has_side_effects=True, vmem_limit_bytes=32 << 20),
        name="exchange",
    )(counts, inputs, cotangent, seed_values.T)

    rows = 256 if d % 256 == 0 else LANES
    new_error, qt = pl.pallas_call(
        error_kernel,
        grid=(d // rows,),
        out_shape=(jax.ShapeDtypeStruct((d, f), BF16), jax.ShapeDtypeStruct((rank, f), F32)),
        in_specs=[
            smem,
            pl.BlockSpec((tokens, rows), lambda i: (0, i)),
            pl.BlockSpec((tokens, f), lambda i: (0, 0)),
            pl.BlockSpec((6 * rank, rows), lambda i: (0, i)),
            pl.BlockSpec((6 * rank, f), lambda i: (0, 0)),
            pl.BlockSpec((8, LANES), lambda i: (0, 0)),
            pl.BlockSpec((rank, f), lambda i: (0, 0)),
        ],
        out_specs=(pl.BlockSpec((rows, f), lambda i: (i, 0)), pl.BlockSpec((rank, f), lambda i: (0, 0))),
        scratch_shapes=[pltpu.VMEM((tokens, f), BF16)],
        compiler_params=pltpu.CompilerParams(vmem_limit_bytes=32 << 20),
        name="error",
    )(counts, inputs, cotangent, basis, qcat, scale, qt)
    return (new_error[None], qt.T)


def solution(mesh):
    return jax.shard_map(
        shards,
        mesh=mesh,
        in_specs=(P("dp", None), P("dp", "tensor"), P("tensor", None), P("dp")),
        out_specs=(P("dp", None, "tensor"), P("tensor", None)),
        check_vma=False,
    )
```

time: 703 us -> 62.1 us (0.09)
  waiting for transfers between devices: 343 us -> 0 us
  matrix products: 244 us -> 0 us
  Pallas kernels: 0 us -> 56.5 us
  local copies, waits for them, and re-layouts: 56.2 us -> 4.12 us
  loops' own time: 22.7 us -> 0 us
  blocking collectives: 15.1 us -> 0 us
  between operations: 15.5 us -> 1.3 us
    psum x2 -> x0, waiting for transfers between devices: 343 us -> none  [the longest x1 234 us: shards(): p_summed = lax.psum(p_local, ('dp', 'tensor'))]
    dot_general x132 -> x0, matrix products: 244 us -> none  [the longest x64 102 us: orth_step(): column = column - jnp.dot(current, coeffs, precision=lax.Precision.HIGHEST)]
    pallas_call x0 -> x2, Pallas kernels: none -> 56.5 us  [the longest x1 45.8 us: shards(): pl.pallas_call(functools.partial(exchange_kernel, n, nz, pitch_p, pitch_w...]
    dynamic_update_slice x32 -> x0, local copies, waits for them, and re-layouts: 49.8 us -> none  [orth_step(): return lax.dynamic_update_slice_in_dim(current, column, column_index, 1)]
    another operation x1 -> x0, loops' own time: 22.7 us -> none  [orthonormal(): return lax.fori_loop(0, cols, orth_step, matrix)]
    psum x1 -> x0, blocking collectives: 15.1 us -> none  [shards(): token_count = lax.psum(counts[0], 'dp').astype(jnp.float32)]
  transfers between devices with their start and end apart: 2 -> 0, of which waited for: 2 -> 0; matrix products, arithmetic and copies ran while one was open for 0% -> 0% of each run, Pallas kernels for 0% -> 0%
where the time goes in v1:
time: 62.1 us; the launch traced here: 61.9 us
  Pallas kernels  56.5 us (91%)
  local copies, waits for them, and re-layouts  4.12 us (7%)
  between operations  1.3 us (2%)
    pallas_call x1, Pallas kernels, shards(): pl.pallas_call(functools.partial(exchange_kernel, n, nz, pitch_p, pitch_w...  45.8 us
    pallas_call x1, Pallas kernels, shards(): pl.pallas_call(error_kernel, grid=(d // rows,), out_shape=(jax.ShapeDtype...  10.8 us
    unnamed x6, local copies, waits for them, and re-layouts  4.12 us

profile of v1, /device:TPU:1, one launch (start us, length us, event | category | flops | bytes accessed | tf_op | source)
XLA Modules:
  0.0 61.9 jit_solution(14389018382306656006)
XLA Ops:
  1.3 0.0 copy-start
  1.3 1.7 %copy-done = bf16[512,2560]{1,0:T(8,128)(2,1)S(1)} copy-done((bf16[512,2560]{1,0:T(8,128)(2,1)S(1)}, bf16[512,2560]{1,0:T(8,128)(2,1)}, u32[]{:S(2)}) %copy-start) | copy-done | bytes 2621464
  3.0 0.0 copy-start.1
  3.0 1.5 %copy-done.1 = bf16[512,1664]{1,0:T(8,128)(2,1)S(1)} copy-done((bf16[512,1664]{1,0:T(8,128)(2,1)S(1)}, bf16[512,1664]{1,0:T(8,128)(2,1)}, u32[]{:S(2)}) %copy-start.1) | copy-done | bytes 1703960
  4.5 0.0 copy-start.2
  4.5 0.9 %copy-done.2 = s32[1664,32]{0,1:T(8,128)S(1)} copy-done((s32[1664,32]{0,1:T(8,128)S(1)}, s32[1664,32]{0,1:T(8,128)}, u32[]{:S(2)}) %copy-start.2) | copy-done | bytes 213016
  5.4 45.8 %exchange.1 = (bf16[192,2560]{1,0:T(8,128)(2,1)S(1)}, bf16[192,1664]{1,0:T(8,128)(2,1)S(1)}, f32[32,1664]{1,0:T(8,128)S(1)}, f32[8,128]{1,0:T(8,128)S(1)}) custom-call(s32[1]{0:T(128)S(6)} %copy.6.count_ref, bf16[512,2560]{1,0:T(8,128)(2,1)S(1)} %copy-done, bf16[512,1664]{1,0:T(8,128)(2,1)S(1)} %copy-done.1, s32[32,1664]{1,0:T(8,128)S(1)} %bitcast.3), custom_call_target="tpu_custom_call" | custom-call | tf_op jit(solution)/shard_map/exchange/pallas_call | solution.py:197
  51.2 10.8 %error.1 = (bf16[2560,1664]{1,0:T(8,128)(2,1)}, f32[32,1664]{1,0:T(8,128)}) custom-call(s32[1]{0:T(128)S(6)} %copy.6.count_ref, bf16[512,2560]{1,0:T(8,128)(2,1)S(1)} %copy-done, bf16[512,1664]{1,0:T(8,128)(2,1)S(1)} %copy-done.1, bf16[192,2560]{1,0:T(8,128)(2,1)S(1)} %get-tuple-element.8.basis_ref, bf16[192,1664]{1,0:T(8,128)(2,1)S(1)} %get-tuple-element.9.qcat_ref, ...), custom_call_target="tpu_custom_call" | custom-call | tf_op jit(solution)/shard_map/error/pallas_call | solution.py:228
Async XLA Ops:
  1.3 1.7 %copy-start = (bf16[512,2560]{1,0:T(8,128)(2,1)S(1)}, bf16[512,2560]{1,0:T(8,128)(2,1)}, u32[]{:S(2)}) copy-start(bf16[512,2560]{1,0:T(8,128)(2,1)} %x_ref.1) | copy-start | bytes 7864324
  3.0 1.5 %copy-start.1 = (bf16[512,1664]{1,0:T(8,128)(2,1)S(1)}, bf16[512,1664]{1,0:T(8,128)(2,1)}, u32[]{:S(2)}) copy-start(bf16[512,1664]{1,0:T(8,128)(2,1)} %c_ref.1) | copy-start | bytes 5111812
  4.5 0.9 %copy-start.2 = (s32[1664,32]{0,1:T(8,128)S(1)}, s32[1664,32]{0,1:T(8,128)}, u32[]{:S(2)}) copy-start(s32[1664,32]{0,1:T(8,128)} %param.6) | copy-start | bytes 638980

commit v2 on v1

v2 whole, which is shorter than its diff:
```python
import functools
import math

import jax
import jax.numpy as jnp
from jax import lax
from jax.experimental import pallas as pl
from jax.experimental.pallas import tpu as pltpu
from jax.sharding import PartitionSpec as P

F32, BF16 = jnp.float32, jnp.bfloat16
LANES = 128
NT = (((1,), (1,)), ((), ()))
TN = (((0,), (0,)), ((), ()))


def round_up(value, unit):
    return -(-value // unit) * unit


def split3(value):
    high = value.astype(BF16)
    rest = value - high.astype(F32)
    mid = rest.astype(BF16)
    low = (rest - mid.astype(F32)).astype(BF16)
    return high, mid, low


def fold3(stacked):
    rows = stacked.shape[0] // 3
    return stacked[:rows] + stacked[rows : 2 * rows] + stacked[2 * rows :]


def exact_dot(left, right, dims=(((1,), (0,)), ((), ()))):
    return lax.dot_general(left, right, dims, precision=lax.Precision.HIGHEST, preferred_element_type=F32)


def inverse_cholesky(gram, group=8):
    size = gram.shape[0]
    row = lax.broadcasted_iota(jnp.int32, (size, size), 0)
    col = lax.broadcasted_iota(jnp.int32, (size, size), 1)
    below = lax.broadcasted_iota(jnp.int32, (size, 1), 0)
    diagonal = jnp.sum(jnp.where(row == col, gram, 0.0), axis=1, keepdims=True)
    floors = jnp.broadcast_to(1e-6 * diagonal, (size, size))
    left, right, scale = gram, (row == col).astype(F32), jnp.ones((size, size), F32)
    for start in range(0, size, group):
        columns = [jnp.broadcast_to(left[:, start + j : start + j + 1], (size, size)) for j in range(group)]
        for j in range(group):
            k = start + j
            pivot = jnp.maximum(columns[j][k : k + 1, :], floors[k : k + 1, :])
            factor = jnp.where(below > k, columns[j] / pivot, 0.0)
            scale = jnp.where(below == k, pivot, scale)
            for i in range(j + 1, group):
                columns[i] = columns[i] - factor * columns[i][k : k + 1, :]
            left, right = left - factor * left[k : k + 1, :], right - factor * right[k : k + 1, :]
    guess = lax.rsqrt(scale)
    return right * (guess * (1.5 - 0.5 * scale * guess * guess))


def spread(ref, value, pitch):
    rows, width = value.shape
    for j in range(width // LANES):
        ref[pl.ds(j, rows, stride=pitch), :] = value[:, j * LANES : (j + 1) * LANES]


def collect(ref, rows, width, pitch):
    return jnp.concatenate([ref[pl.ds(j, rows, stride=pitch), :] for j in range(width // LANES)], axis=1)


def add_blocks(ref, blocks, pitch, rows):
    total = ref[0:rows, :]
    for i in range(1, blocks):
        total = total + ref[i * pitch : i * pitch + rows, :]
    return total


def ring_distance(step, size):
    return min(step, size - step)


def plane_peers(me, n):
    side = math.isqrt(n // 2)
    y, x, core = me // (2 * side), me // 2 % side, me % 2
    steps = [(dy, dx, dc) for dy in range(side) for dx in range(side) for dc in range(2) if dy or dx or dc]
    steps.sort(key=lambda step: -ring_distance(step[0], side) - ring_distance(step[1], side))
    return [((y + dy) % side * side + (x + dx) % side) * 2 + (core + dc) % 2 for dy, dx, dc in steps]


def line_peers(me, n):
    return [(me + step) % n for step in sorted(range(1, n), key=lambda step: -ring_distance(step, n))]


def exchange_kernel(
    n, nz, rows_p, rows_w, pitch_p, pitch_w, tile,
    count_ref, x_hbm, c_hbm, s_hbm,
    grad_ref, basis_ref, qcat_ref, qt_ref, scale_ref,
    x, c, s, live_c, snd1, rcv1, zsnd, zrcv, pfull, snd2, rcv2, wfull, nearly, whole,
    load_sem, send_sem, recv_sem,
):
    me, mz = lax.axis_index("dp"), lax.axis_index("tensor")
    tokens, d = x.shape
    f = c.shape[1]
    in_plane, in_line = plane_peers(me, n), line_peers(mz, nz)

    loads = [pltpu.make_async_copy(src, dst, load_sem.at[i]) for i, (src, dst) in enumerate(((c_hbm, c), (s_hbm, s), (x_hbm, x)))]
    for load in loads:
        load.start()

    barrier = pltpu.get_barrier_semaphore()
    for axis, peers in (("tensor", in_line), ("dp", in_plane)):
        for peer in peers:
            pl.semaphore_signal(barrier, inc=1, device_id={axis: peer}, device_id_type=pl.DeviceIdType.MESH)

    def block(ref, index, pitch, rows):
        return ref.at[pl.ds(pl.multiple_of(index * pitch, 8), rows), :]

    def send(phase, axis, peers, source, target):
        for peer in peers:
            pltpu.make_async_remote_copy(
                src_ref=source(peer), dst_ref=target, send_sem=send_sem.at[phase], recv_sem=recv_sem.at[phase],
                device_id={axis: peer}, device_id_type=pl.DeviceIdType.MESH,
            ).start()

    def wait(sem, ref, rows):
        part = ref.at[pl.ds(0, rows), :]
        pltpu.make_async_copy(part, part, sem).wait()

    def weight_grad(first, last):
        @pl.loop(first, last)
        def _(i):
            here = pl.ds(pl.multiple_of(i * tile, tile), tile)
            grad_ref[here, :] = lax.dot_general(x[:, here], live_c[...], TN, preferred_element_type=F32)

    live = lax.broadcasted_iota(jnp.int32, (n, tokens), 1) < count_ref[0]
    own_p, own_w = pl.ds(pl.multiple_of(me * pitch_p, 8), rows_p), pl.ds(pl.multiple_of(me * pitch_w, 8), rows_w)
    tiles = d // tile

    loads[0].wait()
    loads[1].wait()
    narrow = lax.dot_general((s[...].astype(F32) / 64.0).astype(BF16), c[...], NT, preferred_element_type=F32)
    narrow = jnp.concatenate(split3(jnp.where(live, narrow, 0.0)), axis=0)
    loads[2].wait()
    spread(snd1, fold3(jnp.dot(narrow, x[...], preferred_element_type=F32)), pitch_p)
    rcv1[own_p, :] = snd1[own_p, :]

    pl.semaphore_wait(barrier, n - 1 + nz - 1)
    send(0, "dp", in_plane, lambda peer: block(snd1, peer, pitch_p, rows_p), block(rcv1, me, pitch_p, rows_p))
    position = lax.broadcasted_iota(jnp.int32, live_c.shape, 0)
    live_c[...] = jnp.where(position < count_ref[0], c[...], jnp.zeros_like(c))
    weight_grad(0, tiles // 2)
    wait(recv_sem.at[0], rcv1, (n - 1) * rows_p)

    mine = add_blocks(rcv1, n, pitch_p, rows_p)
    zsnd[...] = mine
    zrcv[pl.ds(pl.multiple_of(mz * pitch_p, 8), rows_p), :] = mine
    send(1, "tensor", in_line, lambda peer: zsnd, block(zrcv, mz, pitch_p, rows_p))
    weight_grad(tiles // 2, tiles)
    wait(recv_sem.at[1], zrcv, (nz - 1) * rows_p)

    pfull[own_p, :] = add_blocks(zrcv, nz, pitch_p, rows_p)
    send(2, "dp", in_plane, lambda peer: block(pfull, me, pitch_p, rows_p), block(pfull, me, pitch_p, rows_p))
    wait(recv_sem.at[2], pfull, (n - 1) * rows_p)

    left = collect(pfull, n, d, pitch_p)
    projected = fold3(lax.dot_general(jnp.concatenate(split3(left), axis=0), x[...], NT, preferred_element_type=F32))
    projected = jnp.concatenate(split3(jnp.where(live, projected, 0.0)), axis=0)
    spread(snd2, fold3(jnp.dot(projected, c[...], preferred_element_type=F32)), pitch_w)
    snd2[pl.ds(rows_w, n, stride=pitch_w), :] = jnp.full((n, LANES), count_ref[0], jnp.int32).astype(F32)
    counted = pl.ds(pl.multiple_of(me * pitch_w, 8), rows_w + 1)
    rcv2[counted, :] = snd2[counted, :]
    send(3, "dp", in_plane, lambda peer: block(snd2, peer, pitch_w, rows_w + 1), block(rcv2, me, pitch_w, rows_w + 1))

    nearly[...] = left

    def orthonormalize():
        step = inverse_cholesky(exact_dot(nearly[...], nearly[...], NT))
        nearly[...] = exact_dot(step, nearly[...])
        return step

    @pl.when(me >= 0)
    def _():
        once = orthonormalize()
        whole[...] = exact_dot(orthonormalize(), once)

    wait(recv_sem.at[3], rcv2, (n - 1) * (rows_w + 1))
    total = add_blocks(rcv2, n, pitch_w, rows_w + 1)
    token_count = total[rows_w : rows_w + 1, :]
    wfull[own_w, :] = total[0:rows_w, :] / token_count
    send(4, "dp", in_plane, lambda peer: block(wfull, me, pitch_w, rows_w), block(wfull, me, pitch_w, rows_w))

    @pl.when(me >= 0)
    def _():
        whole[...] = exact_dot(orthonormalize(), whole[...])
        h, m, l = split3(nearly[...])
        basis_ref[...] = jnp.concatenate((h, h, m, h, l, m), axis=0).T
        scale_ref[...] = jnp.broadcast_to(float(n) / token_count, scale_ref.shape)

    wait(recv_sem.at[4], wfull, (n - 1) * rows_w)
    q = exact_dot(whole[...], collect(wfull, n, f, pitch_w))
    qt_ref[...] = q
    h, m, l = split3(q)
    qcat_ref[...] = jnp.concatenate((h, m, h, l, h, m), axis=0)

    wait(send_sem.at[0], snd1, (n - 1) * rows_p)
    wait(send_sem.at[1], zrcv, (nz - 1) * rows_p)
    wait(send_sem.at[2], pfull, (n - 1) * rows_p)
    wait(send_sem.at[3], snd2, (n - 1) * (rows_w + 1))
    wait(send_sem.at[4], wfull, (n - 1) * rows_w)


def error_kernel(tile, grad_ref, basis_ref, qcat_ref, qt_in, scale_ref, out_hbm, qt_hbm, out, sem):
    qt_copy = pltpu.make_async_copy(qt_in, qt_hbm, sem.at[1])
    qt_copy.start()

    @pl.loop(0, out.shape[0] // tile)
    def _(i):
        here = pl.ds(pl.multiple_of(i * tile, tile), tile)
        approx = jnp.dot(basis_ref[here, :], qcat_ref[...], preferred_element_type=F32)
        out[here, :] = (grad_ref[here, :] * scale_ref[0:1, 0:1] - approx).astype(BF16)
        pltpu.make_async_copy(out.at[here, :], out_hbm.at[here, :], sem.at[0]).start()

    pltpu.make_async_copy(out, out_hbm, sem.at[0]).wait()
    qt_copy.wait()


def largest_tile(length, limit):
    return max(tile for tile in range(LANES, limit + 1, LANES) if length % tile == 0)


def shards(inputs, cotangent, seed_values, counts):
    n, nz = lax.axis_size("dp"), lax.axis_size("tensor")
    tokens, d = inputs.shape
    f = cotangent.shape[1]
    rank = seed_values.shape[1]
    rows_p, rows_w = d // LANES, f // LANES
    pitch_p, pitch_w = round_up(rows_p, 8), round_up(rows_w + 1, 8)
    smem, hbm, vmem = (pl.BlockSpec(memory_space=space) for space in (pltpu.SMEM, pltpu.HBM, pltpu.VMEM))
    held = [pltpu.with_memory_space_constraint(array, pltpu.HBM) for array in (inputs, cotangent, seed_values.T)]
    parts = pl.pallas_call(
        functools.partial(exchange_kernel, n, nz, rows_p, rows_w, pitch_p, pitch_w, largest_tile(d, 256)),
        out_shape=(
            pltpu.VMEM((d, f), F32),
            pltpu.VMEM((d, 6 * rank), BF16),
            pltpu.VMEM((6 * rank, f), BF16),
            pltpu.VMEM((rank, f), F32),
            pltpu.VMEM((8, LANES), F32),
        ),
        in_specs=[smem, hbm, hbm, hbm],
        out_specs=(vmem,) * 5,
        scratch_shapes=[
            pltpu.VMEM((tokens, d), BF16),
            pltpu.VMEM((tokens, f), BF16),
            pltpu.VMEM((rank, f), jnp.int32),
            pltpu.VMEM((tokens, f), BF16),
            pltpu.VMEM((n * pitch_p, LANES), F32),
            pltpu.VMEM((n * pitch_p, LANES), F32),
            pltpu.VMEM((rows_p, LANES), F32),
            pltpu.VMEM((nz * pitch_p, LANES), F32),
            pltpu.VMEM((n * pitch_p, LANES), F32),
            pltpu.VMEM((n * pitch_w, LANES), F32),
            pltpu.VMEM((n * pitch_w, LANES), F32),
            pltpu.VMEM((n * pitch_w, LANES), F32),
            pltpu.VMEM((rank, d), F32),
            pltpu.VMEM((rank, rank), F32),
            pltpu.SemaphoreType.DMA((3,)),
            pltpu.SemaphoreType.DMA((5,)),
            pltpu.SemaphoreType.DMA((5,)),
        ],
        compiler_params=pltpu.CompilerParams(collective_id=0, has_side_effects=True, vmem_limit_bytes=20 << 20),
        name="exchange",
    )(counts, *held)

    new_error, qt = pl.pallas_call(
        functools.partial(error_kernel, largest_tile(d, 640)),
        out_shape=(jax.ShapeDtypeStruct((d, f), BF16), jax.ShapeDtypeStruct((rank, f), F32)),
        in_specs=[vmem] * 5,
        out_specs=(hbm, hbm),
        scratch_shapes=[pltpu.VMEM((d, f), BF16), pltpu.SemaphoreType.DMA((2,))],
        compiler_params=pltpu.CompilerParams(vmem_limit_bytes=18 << 20),
        name="error",
    )(*parts)
    return (new_error[None], qt.T)


def solution(mesh):
    return jax.shard_map(
        shards,
        mesh=mesh,
        in_specs=(P("dp", None), P("dp", "tensor"), P("tensor", None), P("dp")),
        out_specs=(P("dp", None, "tensor"), P("tensor", None)),
        check_vma=False,
    )
```

time: 62.1 us -> 46.4 us (0.75)
  Pallas kernels: 56.5 us -> 45.1 us
  local copies, waits for them, and re-layouts: 4.12 us -> 0 us
    pallas_call x2, Pallas kernels: 56.5 us -> 45.1 us  [the longest x1 40.6 us: shards(): pl.pallas_call(functools.partial(exchange_kernel, n, nz, rows_p, rows_w,...]
    unnamed x6 -> x0, local copies, waits for them, and re-layouts: 4.12 us -> none
where the time goes in v2:
time: 46.4 us; the launch traced here: 46.3 us
  Pallas kernels  45.1 us (97%)
  between operations  1.28 us (3%)
    pallas_call x1, Pallas kernels, shards(): pl.pallas_call(functools.partial(exchange_kernel, n, nz, rows_p, rows_w,...  40.6 us
    pallas_call x1, Pallas kernels, shards(): pl.pallas_call(functools.partial(error_kernel, largest_tile(d, 640)), out...  4.42 us

profile of v2, /device:TPU:1, one launch (start us, length us, event | category | flops | bytes accessed | tf_op | source)
XLA Modules:
  0.0 46.3 jit_solution(7669757271722138851)
XLA Ops:
  1.3 40.6 %exchange.1 = (f32[2560,1664]{1,0:T(8,128)S(1)}, bf16[2560,192]{1,0:T(8,128)(2,1)S(1)}, bf16[192,1664]{1,0:T(8,128)(2,1)S(1)}, f32[32,1664]{1,0:T(8,128)S(1)}, f32[8,128]{1,0:T(8,128)S(1)}) custom-call(s32[1]{0:T(128)S(6)} %copy.6.count_ref, bf16[512,2560]{1,0:T(8,128)(2,1)} %x_hbm.1, bf16[512,1664]{1,0:T(8,128)(2,1)} %c_hbm.1, s32[32,1664]{1,0:T(8,128)} %bitcast.3), custom_call_target="tpu_custom_call" | custom-call | tf_op jit(solution)/shard_map/exchange/pallas_call | solution.py:239
  41.9 4.4 %error.1 = (bf16[2560,1664]{1,0:T(8,128)(2,1)}, f32[32,1664]{1,0:T(8,128)}) custom-call(f32[2560,1664]{1,0:T(8,128)S(1)} %get-tuple-element.9.grad_ref, bf16[2560,192]{1,0:T(8,128)(2,1)S(1)} %get-tuple-element.10.basis_ref, bf16[192,1664]{1,0:T(8,128)(2,1)S(1)} %get-tuple-element.11.qcat_ref, f32[32,1664]{1,0:T(8,128)S(1)} %get-tuple-element.12.qt_in, ...), custom_call_target="tpu_custom_call" | custom-call | tf_op jit(solution)/shard_map/error/pallas_call | solution.py:273

commit v3 on v2

v3 whole, which is shorter than its diff:
```python
import functools
import math

import jax
import jax.numpy as jnp
from jax import lax
from jax.experimental import pallas as pl
from jax.experimental.pallas import tpu as pltpu
from jax.sharding import PartitionSpec as P

F32, BF16 = jnp.float32, jnp.bfloat16
LANES = 128
NT = (((1,), (1,)), ((), ()))
TN = (((0,), (0,)), ((), ()))


def round_up(value, unit):
    return -(-value // unit) * unit


def split3(value):
    high = value.astype(BF16)
    rest = value - high.astype(F32)
    mid = rest.astype(BF16)
    low = (rest - mid.astype(F32)).astype(BF16)
    return high, mid, low


def fold3(stacked):
    rows = stacked.shape[0] // 3
    return stacked[:rows] + stacked[rows : 2 * rows] + stacked[2 * rows :]


def exact_dot(left, right, dims=(((1,), (0,)), ((), ()))):
    return lax.dot_general(left, right, dims, precision=lax.Precision.HIGHEST, preferred_element_type=F32)


def inverse_cholesky(gram, group=8):
    size = gram.shape[0]
    row = lax.broadcasted_iota(jnp.int32, (size, size), 0)
    col = lax.broadcasted_iota(jnp.int32, (size, size), 1)
    below = lax.broadcasted_iota(jnp.int32, (size, 1), 0)
    diagonal = jnp.sum(jnp.where(row == col, gram, 0.0), axis=1, keepdims=True)
    floors = jnp.broadcast_to(1e-6 * diagonal, (size, size))
    left, right, scale = gram, (row == col).astype(F32), jnp.ones((size, size), F32)
    for start in range(0, size, group):
        columns = [jnp.broadcast_to(left[:, start + j : start + j + 1], (size, size)) for j in range(group)]
        for j in range(group):
            k = start + j
            pivot = jnp.maximum(columns[j][k : k + 1, :], floors[k : k + 1, :])
            factor = jnp.where(below > k, columns[j] / pivot, 0.0)
            scale = jnp.where(below == k, pivot, scale)
            for i in range(j + 1, group):
                columns[i] = columns[i] - factor * columns[i][k : k + 1, :]
            left, right = left - factor * left[k : k + 1, :], right - factor * right[k : k + 1, :]
    guess = lax.rsqrt(scale)
    return right * (guess * (1.5 - 0.5 * scale * guess * guess))


def spread(ref, value, pitch, first):
    rows, width = value.shape
    for j in range(width // LANES):
        ref[pl.ds(first + j, rows, stride=pitch), :] = value[:, j * LANES : (j + 1) * LANES]


def collect(ref, rows, pitch, part):
    return jnp.concatenate([ref[pl.ds(j, rows, stride=pitch), :] for j in range(*part)], axis=1)


def add_blocks(ref, blocks, pitch, part):
    total = ref[part[0] : part[1], :]
    for i in range(1, blocks):
        total = total + ref[i * pitch + part[0] : i * pitch + part[1], :]
    return total


def lanes(part):
    return pl.ds(part[0] * LANES, (part[1] - part[0]) * LANES)


def ring_distance(step, size):
    return min(step, size - step)


def plane_peers(me, n):
    side = math.isqrt(n // 2)
    y, x, core = me // (2 * side), me // 2 % side, me % 2
    steps = [(dy, dx, dc) for dy in range(side) for dx in range(side) for dc in range(2) if dy or dx or dc]
    far = [-ring_distance(step, side) for step in range(side)]
    steps.sort(key=lambda step: (far[step[0]] + far[step[1]], step[2], (3 * step[0] + 5 * step[1]) % side))
    return [((y + dy) % side * side + (x + dx) % side) * 2 + (core + dc) % 2 for dy, dx, dc in steps]


def line_peers(me, n):
    return [(me + step) % n for step in sorted(range(1, n), key=lambda step: -ring_distance(step, n))]


def exchange_kernel(
    n, nz, parts_p, parts_w, pitch_p, pitch_w, tile,
    count_ref, x_hbm, c_hbm, s_hbm,
    grad_ref, basis_ref, wcat_ref, w_ref, whole_ref, scale_ref,
    x, c, s, live_c, snd1a, snd1b, rcv1, zsnd, zrcv, pfulla, pfullb, snd2, rcv2, wfull, nearly, whole,
    load_sem, send_sem, recv_sem,
):
    me, mz = lax.axis_index("dp"), lax.axis_index("tensor")
    snd1, pfull = (snd1a, snd1b), (pfulla, pfullb)
    tokens, d = x.shape
    in_plane, in_line = plane_peers(me, n), line_peers(mz, nz)

    pairs = [(s_hbm, s), (c_hbm, c)] + [(x_hbm.at[:, lanes(part)], x.at[:, lanes(part)]) for part in parts_p]
    loads = [pltpu.make_async_copy(src, dst, load_sem.at[i]) for i, (src, dst) in enumerate(pairs)]
    for load in loads:
        load.start()

    barrier = pltpu.get_barrier_semaphore()
    for axis, peers in (("dp", in_plane), ("tensor", in_line)):
        for peer in peers:
            pl.semaphore_signal(barrier, inc=1, device_id={axis: peer}, device_id_type=pl.DeviceIdType.MESH)

    def rows_of(index, pitch, part):
        return pl.ds(index * pitch + part[0], part[1] - part[0])

    def send(phase, half, axis, peers, source, target):
        for peer in peers:
            pltpu.make_async_remote_copy(
                src_ref=source(peer), dst_ref=target, send_sem=send_sem.at[phase, half], recv_sem=recv_sem.at[phase, half],
                device_id={axis: peer}, device_id_type=pl.DeviceIdType.MESH,
            ).start()

    def wait(sem, ref, peers, part):
        here = ref.at[pl.ds(0, len(peers) * (part[1] - part[0])), :]
        pltpu.make_async_copy(here, here, sem).wait()

    def weight_grad(first, last):
        @pl.loop(first, last)
        def _(i):
            here = pl.ds(pl.multiple_of(i * tile, tile), tile)
            grad_ref[here, :] = lax.dot_general(x[:, here], live_c[...], TN, preferred_element_type=F32)

    live = lax.broadcasted_iota(jnp.int32, (n, tokens), 1) < count_ref[0]
    tiles = d // tile
    pitches_p = [round_up(part[1] - part[0], 8) for part in parts_p]
    counted_w = parts_w[:-1] + [(parts_w[-1][0], parts_w[-1][1] + 1)]

    loads[0].wait()
    loads[1].wait()
    narrow = lax.dot_general((s[...].astype(F32) / 64.0).astype(BF16), c[...], NT, preferred_element_type=F32)
    narrow = jnp.concatenate(split3(jnp.where(live, narrow, 0.0)), axis=0)
    for half, part in enumerate(parts_p):
        loads[2 + half].wait()
        spread(snd1[half], fold3(jnp.dot(narrow, x[:, lanes(part)], preferred_element_type=F32)), pitches_p[half], 0)
        rcv1[rows_of(me, pitch_p, part), :] = snd1[half][pl.ds(me * pitches_p[half], part[1] - part[0]), :]
        if half == 0:
            pl.semaphore_wait(barrier, n - 1 + nz - 1)
        send(0, half, "dp", in_plane, lambda peer: snd1[half].at[pl.ds(peer * pitches_p[half], part[1] - part[0]), :], rcv1.at[rows_of(me, pitch_p, part), :])
    position = lax.broadcasted_iota(jnp.int32, live_c.shape, 0)
    live_c[...] = jnp.where(position < count_ref[0], c[...], jnp.zeros_like(c))
    weight_grad(0, tiles // 2)

    for half, part in enumerate(parts_p):
        wait(recv_sem.at[0, half], rcv1, in_plane, part)
        mine = add_blocks(rcv1, n, pitch_p, part)
        zsnd[rows_of(0, pitch_p, part), :] = mine
        zrcv[rows_of(mz, pitch_p, part), :] = mine
        send(1, half, "tensor", in_line, lambda peer: zsnd.at[rows_of(0, pitch_p, part), :], zrcv.at[rows_of(mz, pitch_p, part), :])
    weight_grad(tiles // 2, tiles)

    for half, part in enumerate(parts_p):
        wait(recv_sem.at[1, half], zrcv, in_line, part)
        mine = pfull[half].at[pl.ds(me * pitches_p[half], part[1] - part[0]), :]
        mine[...] = add_blocks(zrcv, nz, pitch_p, part)
        send(2, half, "dp", in_plane, lambda peer: mine, mine)

    projected = 0.0
    for half, part in enumerate(parts_p):
        wait(recv_sem.at[2, half], pfull[half], in_plane, part)
        left = collect(pfull[half], n, pitches_p[half], (0, part[1] - part[0]))
        nearly[:, lanes(part)] = left
        projected = projected + lax.dot_general(
            jnp.concatenate(split3(left), axis=0), x[:, lanes(part)], NT, preferred_element_type=F32
        )
    projected = jnp.concatenate(split3(jnp.where(live, fold3(projected), 0.0)), axis=0)
    snd2[pl.ds(parts_w[-1][1], n, stride=pitch_w), :] = jnp.full((n, LANES), count_ref[0], jnp.int32).astype(F32)
    spread(snd2, fold3(jnp.dot(projected, c[...], preferred_element_type=F32)), pitch_w, 0)
    for half, part in enumerate(counted_w):
        rcv2[rows_of(me, pitch_w, part), :] = snd2[rows_of(me, pitch_w, part), :]
        send(3, half, "dp", in_plane, lambda peer: snd2.at[rows_of(peer, pitch_w, part), :], rcv2.at[rows_of(me, pitch_w, part), :])

    def orthonormalize():
        step = inverse_cholesky(exact_dot(nearly[...], nearly[...], NT))
        nearly[...] = exact_dot(step, nearly[...])
        return step

    @pl.when(me >= 0)
    def _():
        once = orthonormalize()
        whole[...] = exact_dot(orthonormalize(), once)

    for half, part in enumerate(parts_w):
        wait(recv_sem.at[3, half], rcv2, in_plane, counted_w[half])
        total = add_blocks(rcv2, n, pitch_w, counted_w[half])
        here = rows_of(me, pitch_w, part)
        wfull[here, :] = total[0 : part[1] - part[0], :]
        send(4, half, "dp", in_plane, lambda peer: wfull.at[here, :], wfull.at[here, :])
    token_count = total[part[1] - part[0] :, :]

    @pl.when(me >= 0)
    def _():
        upper = exact_dot(orthonormalize(), whole[...]) / token_count[:, 0:1]
        whole_ref[...] = upper
        h, m, l = split3(exact_dot(upper, nearly[...], TN))
        basis_ref[...] = jnp.concatenate((h, h, m, h, l, m), axis=0).T
        scale_ref[...] = jnp.broadcast_to(float(n) / token_count, scale_ref.shape)

    for half, part in enumerate(parts_w):
        wait(recv_sem.at[4, half], wfull, in_plane, part)
        w = collect(wfull, n, pitch_w, part)
        w_ref[:, lanes(part)] = w
        h, m, l = split3(w)
        wcat_ref[:, lanes(part)] = jnp.concatenate((h, m, h, l, h, m), axis=0)

    for phase, peers, parts in ((0, in_plane, parts_p), (1, in_line, parts_p), (2, in_plane, parts_p), (3, in_plane, counted_w), (4, in_plane, parts_w)):
        for half, part in enumerate(parts):
            wait(send_sem.at[phase, half], rcv1, peers, part)


def error_kernel(tile, grad_ref, basis_ref, wcat_ref, w_ref, whole_ref, scale_ref, out_hbm, qt_hbm, out, qt, sem):
    @pl.loop(0, out.shape[0] // tile)
    def _(i):
        here = pl.ds(pl.multiple_of(i * tile, tile), tile)
        approx = jnp.dot(basis_ref[here, :], wcat_ref[...], preferred_element_type=F32)
        out[here, :] = (grad_ref[here, :] * scale_ref[0:1, 0:1] - approx).astype(BF16)
        pltpu.make_async_copy(out.at[here, :], out_hbm.at[here, :], sem.at[0]).start()

    qt[...] = exact_dot(whole_ref[...], w_ref[...])
    qt_copy = pltpu.make_async_copy(qt, qt_hbm, sem.at[1])
    qt_copy.start()
    pltpu.make_async_copy(out, out_hbm, sem.at[0]).wait()
    qt_copy.wait()


def halves(rows, first):
    return [(0, first), (first, rows)]


def largest_tile(length, limit):
    return max(tile for tile in range(LANES, limit + 1, LANES) if length % tile == 0)


def shards(inputs, cotangent, seed_values, counts):
    n, nz = lax.axis_size("dp"), lax.axis_size("tensor")
    tokens, d = inputs.shape
    f = cotangent.shape[1]
    rank = seed_values.shape[1]
    rows_p, rows_w = d // LANES, f // LANES
    pitch_p, pitch_w = round_up(rows_p, 8), round_up(rows_w + 1, 8)
    parts_p, parts_w = halves(rows_p, max(1, rows_p * 2 // 5)), [(0, rows_w)]
    smem, hbm, vmem = (pl.BlockSpec(memory_space=space) for space in (pltpu.SMEM, pltpu.HBM, pltpu.VMEM))
    held = [pltpu.with_memory_space_constraint(array, pltpu.HBM) for array in (inputs, cotangent, seed_values.T)]
    parts = pl.pallas_call(
        functools.partial(exchange_kernel, n, nz, parts_p, parts_w, pitch_p, pitch_w, largest_tile(d, 256)),
        out_shape=(
            pltpu.VMEM((d, f), F32),
            pltpu.VMEM((d, 6 * rank), BF16),
            pltpu.VMEM((6 * rank, f), BF16),
            pltpu.VMEM((rank, f), F32),
            pltpu.VMEM((rank, rank), F32),
            pltpu.VMEM((8, LANES), F32),
        ),
        in_specs=[smem, hbm, hbm, hbm],
        out_specs=(vmem,) * 6,
        scratch_shapes=[
            pltpu.VMEM((tokens, d), BF16),
            pltpu.VMEM((tokens, f), BF16),
            pltpu.VMEM((rank, f), jnp.int32),
            pltpu.VMEM((tokens, f), BF16),
            *[pltpu.VMEM(((n + 1) * round_up(part[1] - part[0], 8), LANES), F32) for part in parts_p],
            pltpu.VMEM((n * pitch_p, LANES), F32),
            pltpu.VMEM((pitch_p, LANES), F32),
            pltpu.VMEM((nz * pitch_p, LANES), F32),
            *[pltpu.VMEM(((n + 1) * round_up(part[1] - part[0], 8), LANES), F32) for part in parts_p],
            pltpu.VMEM(((n + 1) * pitch_w, LANES), F32),
            pltpu.VMEM(((n + 1) * pitch_w, LANES), F32),
            pltpu.VMEM(((n + 1) * pitch_w, LANES), F32),
            pltpu.VMEM((rank, d), F32),
            pltpu.VMEM((rank, rank), F32),
            pltpu.SemaphoreType.DMA((4,)),
            pltpu.SemaphoreType.DMA((5, 2)),
            pltpu.SemaphoreType.DMA((5, 2)),
        ],
        compiler_params=pltpu.CompilerParams(collective_id=0, has_side_effects=True, vmem_limit_bytes=20 << 20),
        name="exchange",
    )(counts, *held)

    new_error, qt = pl.pallas_call(
        functools.partial(error_kernel, largest_tile(d, 640)),
        out_shape=(jax.ShapeDtypeStruct((d, f), BF16), jax.ShapeDtypeStruct((rank, f), F32)),
        in_specs=[vmem] * 6,
        out_specs=(hbm, hbm),
        scratch_shapes=[pltpu.VMEM((d, f), BF16), pltpu.VMEM((rank, f), F32), pltpu.SemaphoreType.DMA((2,))],
        compiler_params=pltpu.CompilerParams(vmem_limit_bytes=18 << 20),
        name="error",
    )(*parts)
    return (new_error[None], qt.T)


def solution(mesh):
    return jax.shard_map(
        shards,
        mesh=mesh,
        in_specs=(P("dp", None), P("dp", "tensor"), P("tensor", None), P("dp")),
        out_specs=(P("dp", None, "tensor"), P("tensor", None)),
        check_vma=False,
    )
```

time: 46.4 us -> 45.4 us (0.978)
  Pallas kernels: 45.1 us -> 44 us
    pallas_call x1, Pallas kernels: 40.6 us -> 39.6 us  [shards(): pl.pallas_call(functools.partial(exchange_kernel, n, nz, parts_p, parts_w...]
where the time goes in v3:
time: 45.4 us; the launch traced here: 45.3 us
  Pallas kernels  44 us (97%)
  between operations  1.28 us (3%)
    pallas_call x1, Pallas kernels, shards(): pl.pallas_call(functools.partial(exchange_kernel, n, nz, parts_p, parts_w...  39.6 us
    pallas_call x1, Pallas kernels, shards(): pl.pallas_call(functools.partial(error_kernel, largest_tile(d, 640)), out...  4.41 us

profile of v3, /device:TPU:1, one launch (start us, length us, event | category | flops | bytes accessed | tf_op | source)
XLA Modules:
  0.0 45.3 jit_solution(18289645680866228863)
XLA Ops:
  1.3 39.6 %exchange.1 = (f32[2560,1664]{1,0:T(8,128)S(1)}, bf16[2560,192]{1,0:T(8,128)(2,1)S(1)}, bf16[192,1664]{1,0:T(8,128)(2,1)S(1)}, f32[32,1664]{1,0:T(8,128)S(1)}, f...) custom-call(s32[1]{0:T(128)S(6)} %copy.6.count_ref, bf16[512,2560]{1,0:T(8,128)(2,1)} %x_hbm.1, bf16[512,1664]{1,0:T(8,128)(2,1)} %c_hbm.1, ...), custom_call_target="tpu_custom_call" | custom-call | tf_op jit(solution)/shard_map/exchange/pallas_call | solution.py:260
  40.9 4.4 %error.1 = (bf16[2560,1664]{1,0:T(8,128)(2,1)}, f32[32,1664]{1,0:T(8,128)}) custom-call(f32[2560,1664]{1,0:T(8,128)S(1)} %get-tuple-element.10.grad_ref, bf16[2560,192]{1,0:T(8,128)(2,1)S(1)} %get-tuple-element.11.basis_ref, bf16[192,1664]{1,0:T(8,128)(2,1)S(1)} %get-tuple-element.12.wcat_ref, f32[32,1664]{1,0:T(8,128)S(1)} %get-tuple-element.13.w_ref, ...), custom_call_target="tpu_custom_call" | custom-call | tf_op jit(solution)/shard_map/error/pallas_call | solution.py:295

commit v4 on v3

--- a/solution.py
+++ b/solution.py
@@ -107,15 +107,15 @@
     tokens, d = x.shape
     in_plane, in_line = plane_peers(me, n), line_peers(mz, nz)
 
+    barrier = pltpu.get_barrier_semaphore()
+    for axis, peers in (("dp", in_plane), ("tensor", in_line)):
+        for peer in peers:
+            pl.semaphore_signal(barrier, inc=1, device_id={axis: peer}, device_id_type=pl.DeviceIdType.MESH)
+
     pairs = [(s_hbm, s), (c_hbm, c)] + [(x_hbm.at[:, lanes(part)], x.at[:, lanes(part)]) for part in parts_p]
     loads = [pltpu.make_async_copy(src, dst, load_sem.at[i]) for i, (src, dst) in enumerate(pairs)]
     for load in loads:
         load.start()
-
-    barrier = pltpu.get_barrier_semaphore()
-    for axis, peers in (("dp", in_plane), ("tensor", in_line)):
-        for peer in peers:
-            pl.semaphore_signal(barrier, inc=1, device_id={axis: peer}, device_id_type=pl.DeviceIdType.MESH)
 
     def rows_of(index, pitch, part):
         return pl.ds(index * pitch + part[0], part[1] - part[0])
@@ -149,10 +149,11 @@
     for half, part in enumerate(parts_p):
         loads[2 + half].wait()
         spread(snd1[half], fold3(jnp.dot(narrow, x[:, lanes(part)], preferred_element_type=F32)), pitches_p[half], 0)
-        rcv1[rows_of(me, pitch_p, part), :] = snd1[half][pl.ds(me * pitches_p[half], part[1] - part[0]), :]
         if half == 0:
             pl.semaphore_wait(barrier, n - 1 + nz - 1)
         send(0, half, "dp", in_plane, lambda peer: snd1[half].at[pl.ds(peer * pitches_p[half], part[1] - part[0]), :], rcv1.at[rows_of(me, pitch_p, part), :])
+    for half, part in enumerate(parts_p):
+        rcv1[rows_of(me, pitch_p, part), :] = snd1[half][pl.ds(me * pitches_p[half], part[1] - part[0]), :]
     position = lax.broadcasted_iota(jnp.int32, live_c.shape, 0)
     live_c[...] = jnp.where(position < count_ref[0], c[...], jnp.zeros_like(c))
     weight_grad(0, tiles // 2)
@@ -161,8 +162,8 @@
         wait(recv_sem.at[0, half], rcv1, in_plane, part)
         mine = add_blocks(rcv1, n, pitch_p, part)
         zsnd[rows_of(0, pitch_p, part), :] = mine
+        send(1, half, "tensor", in_line, lambda peer: zsnd.at[rows_of(0, pitch_p, part), :], zrcv.at[rows_of(mz, pitch_p, part), :])
         zrcv[rows_of(mz, pitch_p, part), :] = mine
-        send(1, half, "tensor", in_line, lambda peer: zsnd.at[rows_of(0, pitch_p, part), :], zrcv.at[rows_of(mz, pitch_p, part), :])
     weight_grad(tiles // 2, tiles)
 
     for half, part in enumerate(parts_p):
@@ -183,8 +184,8 @@
     snd2[pl.ds(parts_w[-1][1], n, stride=pitch_w), :] = jnp.full((n, LANES), count_ref[0], jnp.int32).astype(F32)
     spread(snd2, fold3(jnp.dot(projected, c[...], preferred_element_type=F32)), pitch_w, 0)
     for half, part in enumerate(counted_w):
+        send(3, half, "dp", in_plane, lambda peer: snd2.at[rows_of(peer, pitch_w, part), :], rcv2.at[rows_of(me, pitch_w, part), :])
         rcv2[rows_of(me, pitch_w, part), :] = snd2[rows_of(me, pitch_w, part), :]
-        send(3, half, "dp", in_plane, lambda peer: snd2.at[rows_of(peer, pitch_w, part), :], rcv2.at[rows_of(me, pitch_w, part), :])
 
     def orthonormalize():
         step = inverse_cholesky(exact_dot(nearly[...], nearly[...], NT))

time: 45.4 us -> 45.4 us (level)
  no operation moved by 1% of the time
where the time goes in v4:
time: 45.4 us; the launch traced here: 45.3 us
  Pallas kernels  44 us (97%)
  between operations  1.28 us (3%)
    pallas_call x1, Pallas kernels, shards(): pl.pallas_call(functools.partial(exchange_kernel, n, nz, parts_p, parts_w...  39.6 us
    pallas_call x1, Pallas kernels, shards(): pl.pallas_call(functools.partial(error_kernel, largest_tile(d, 640)), out...  4.41 us

profile of v4, /device:TPU:1, one launch (start us, length us, event | category | flops | bytes accessed | tf_op | source)
XLA Modules:
  0.0 45.3 jit_solution(6893784315891182191)
XLA Ops:
  1.3 39.6 %exchange.1 = (f32[2560,1664]{1,0:T(8,128)S(1)}, bf16[2560,192]{1,0:T(8,128)(2,1)S(1)}, bf16[192,1664]{1,0:T(8,128)(2,1)S(1)}, f32[32,1664]{1,0:T(8,128)S(1)}, f...) custom-call(s32[1]{0:T(128)S(6)} %copy.6.count_ref, bf16[512,2560]{1,0:T(8,128)(2,1)} %x_hbm.1, bf16[512,1664]{1,0:T(8,128)(2,1)} %c_hbm.1, ...), custom_call_target="tpu_custom_call" | custom-call | tf_op jit(solution)/shard_map/exchange/pallas_call | solution.py:261
  40.9 4.4 %error.1 = (bf16[2560,1664]{1,0:T(8,128)(2,1)}, f32[32,1664]{1,0:T(8,128)}) custom-call(f32[2560,1664]{1,0:T(8,128)S(1)} %get-tuple-element.10.grad_ref, bf16[2560,192]{1,0:T(8,128)(2,1)S(1)} %get-tuple-element.11.basis_ref, bf16[192,1664]{1,0:T(8,128)(2,1)S(1)} %get-tuple-element.12.wcat_ref, f32[32,1664]{1,0:T(8,128)S(1)} %get-tuple-element.13.w_ref, ...), custom_call_target="tpu_custom_call" | custom-call | tf_op jit(solution)/shard_map/error/pallas_call | solution.py:296
